TPU v7x, 128 devices: a whole 4x4x4 slice. The times are simulated.
128 devices in a mesh: comp: 2 (over z_lo), tile: 64 (over z_hi, x, y, core).
Axes of the slice: x: 4, y: 4, z: 4 (z_hi: 2, z_lo: 2; z = z_hi * 2 + z_lo), core: 2. Of those that a mesh axis runs over, the one named last changes fastest.
Arguments:
- state: float32 [2, 16, 2048, 256], P('comp', None, 'tile'), may hold values from -6 to 6
- weights: bfloat16 [2, 4096, 4, 128, 128], P('comp', 'tile'), may hold values from -0.25 to 0.25
- send_slots: int32 [2, 64, 64, 8], P('comp', 'tile'), may hold values from 0 to 63, as said below
- recv_pos: int32 [2, 4096, 4], P('comp', 'tile'), may hold values from 0 to 511, as said below
- diffusion: float32 [2, 16], P('comp'), may hold values from 0.02 to 0.24
- coupling: float32 [2, 16], P('comp'), may hold values from 0.2 to 1
- sea_mask: int32 [2048, 256], P('tile'), may hold values 0 or 1
Outputs:
- new_state: float32 [2, 16, 2048, 256], P('comp', None, 'tile')
- incoming: float32 [2, 16, 2048, 256], P('comp', None, 'tile')
Inputs may be any that keep to these rules, and one draw needn't show every extreme that they name: `send_slots`: the block of tile s carried in slot j from tile s to tile t for component c's needs. `recv_pos`: slot positions source tile times 8 plus j, all different within one receiving tile; in every receiving tile one source tile fills all its 8 slots.
All inputs are finite; a program needn't handle non-finite values. No bound on the sum of `sea_mask` on one device may be relied on, other than what follows from the above.
Results may differ from a plain program's by a relative error of at most 0.0029.
Values may be sent and summed in bfloat16 or wider, within the bound.
A program may use at most 128 MiB of HBM per device.

v0:
```python
import jax
import jax.numpy as jnp
from jax import lax
from jax.sharding import PartitionSpec as P

FIELDS = 16
ROWS_DEV = 32
COLUMNS = 256
BLOCK = 128
SOURCES = 4
BLOCKS_DEV = 64


def partner(value, axis, distance):
    mask = 2**distance
    pairs = [(source, source ^ mask) for source in range(lax.axis_size(axis))]
    return lax.ppermute(value, axis, pairs)


def with_halo(cells, sides, width):
    for axis, dim in sides:
        count = lax.axis_size(axis)
        head = lax.slice_in_dim(cells, 0, width, axis=dim)
        tail = lax.slice_in_dim(cells, cells.shape[dim] - width, cells.shape[dim], axis=dim)
        cells = jnp.concatenate(
            [
                lax.ppermute(tail, axis, [(i, (i + 1) % count) for i in range(count)]),
                cells,
                lax.ppermute(head, axis, [((i + 1) % count, i) for i in range(count)]),
            ],
            axis=dim,
        )
    return cells


def per_device(state, weights, send_slots, recv_pos, diffusion, coupling, sea_mask):
    field = state[0]
    ocean = lax.axis_index("comp") == 1
    cover = jnp.where(ocean, sea_mask.astype(jnp.float32), jnp.ones_like(sea_mask, jnp.float32))
    surface = field.astype(jnp.bfloat16).reshape(FIELDS, BLOCKS_DEV, BLOCK)
    facing = partner(surface, "comp", 0)
    positions = recv_pos[0].reshape(-1)
    slot_count = send_slots.shape[3]
    blocks, lists = (
        lax.all_gather(facing, "tile", axis=1, tiled=True),
        lax.all_gather(send_slots[0], "tile", axis=0, tiled=True),
    )
    mine = jnp.take(lists, lax.axis_index("tile"), axis=1).reshape(-1)
    source = positions // slot_count * BLOCKS_DEV + jnp.take(mine, positions)
    picked = jnp.take(blocks, source, axis=1)
    picked = picked.reshape(FIELDS, BLOCKS_DEV, SOURCES, BLOCK)
    flux = jnp.einsum("vbkc,bkdc->vbd", picked, weights[0], preferred_element_type=jnp.float32)
    flux = flux.reshape(FIELDS, ROWS_DEV, COLUMNS)
    rates = diffusion[0][:, None, None]
    stepped = field
    for substep in range(2):
        padded = with_halo(stepped.astype(jnp.bfloat16), (("tile", 1),), 1).astype(stepped.dtype)
        laplace = (
            padded[:, 2:, :]
            + padded[:, :-2, :]
            + jnp.roll(stepped, 1, 2)
            + jnp.roll(stepped, -1, 2)
            - 4.0 * stepped
        )
        stepped = stepped + rates * cover * laplace
    result = stepped + coupling[0][:, None, None] * cover * flux
    return (result[None], flux[None])


def solution(mesh):
    return jax.shard_map(
        per_device,
        mesh=mesh,
        in_specs=(
            P("comp", None, "tile", None),
            P("comp", "tile", None, None, None),
            P("comp", "tile", None, None),
            P("comp", "tile", None),
            P("comp", None),
            P("comp", None),
            P("tile", None),
        ),
        out_specs=(P("comp", None, "tile", None), P("comp", None, "tile", None)),
        check_vma=False,
    )
```

profile of v0, /device:TPU:31, one launch (start us, length us, event | category | flops | bytes accessed | tf_op | source)
XLA Modules:
  0.0 158.8 jit_solution(3414080734798790167)
XLA Ops:
  7.2 1.3 fusion.27
  8.6 0.1 convert_element_type.28
  8.7 1.7 %collective-permute-start.4 = (bf16[16,64,128]{2,1,0:T(8,128)(2,1)S(1)}, bf16[16,64,128]{2,1,0:T(8,128)(2,1)S(1)}, u32[]{:S(2)}, u32[]{:S(2)}) collective-permute-start(bf16[16,64,128]{2,1,0:T(8,128)(2,1)S(1)} %convert_element_type.28), channel_id=1, source_target_pairs={{0,64},{64,0},{1,65},{65,1},{2,66},{66,2},{3,67},{67,3},{4,68},{68... | collective-permute-start | bytes 786440 | tf_op jit(solution)/shard_map/ppermute | solution.py:17
  10.4 5.9 %collective-permute-done.4 = bf16[16,64,128]{2,1,0:T(8,128)(2,1)S(1)} collective-permute-done((bf16[16,64,128]{2,1,0:T(8,128)(2,1)S(1)}, bf16[16,64,128]{2,1,0:T(8,128)(2,1)S(1)}, u32[]{:S(2)}, u32[]{:S(2)}) %collective-permute-start.4) | collective-permute-done | bytes 262176 | tf_op jit(solution)/shard_map/ppermute | solution.py:17
  16.3 0.9 copy.28
  17.2 4.3 %collective-permute-start = (bf16[16,1,256]{2,1,0:T(2,128)(2,1)S(1)}, bf16[16,1,256]{2,1,0:T(2,128)(2,1)S(1)}, u32[]{:S(2)}, u32[]{:S(2)}) collective-permute-start(bf16[16,1,256]{2,1,0:T(2,128)(2,1)S(1)} %get-tuple-element.27), channel_id=1, source_target_pairs={{0,1},{1,2},{2,3},{3,4},{4,5},{5,6},{6,7},{7,8},{8,9},{9,10},{10,1... | collective-permute-start | bytes 24584 | tf_op jit(solution)/shard_map/ppermute | solution.py:27
  21.5 92.0 %all-gather = s32[64,1,64,8]{2,3,1,0:T(8,128)S(1)} all-gather(s32[1,1,64,8]{2,3,1,0:T(8,128)} %param.9), channel_id=2, replica_groups=mesh['comp'=2,'tile'=64] {'tile'}, dimensions={0}, use_global_device_ids=true | all-gather | bytes 133120 | tf_op jit(solution)/shard_map/all_gather | solution.py:46
  113.5 1.2 select_reduce_fusion
  114.8 0.1 select_n.103
  114.9 0.8 copy.25
  115.6 0.1 reshape_squeeze.6
  115.8 1.9 %gather_fusion = s32[256]{0:T(256)S(1)} fusion(s32[512]{0:T(512)S(1)} %select_n.103, s32[1024]{0:T(1024)S(1)} %pad_clamp_fusion.1), kind=kCustom, calls=%fused_computation | custom fusion | bytes 3072 | tf_op jit(solution)/shard_map/jit(_take)/gather | solution.py:49
  117.7 0.1 gather.20
  117.8 0.1 copy.26
  117.9 0.7 compare_and_fusion
  118.6 0.8 convert_select_fusion
  119.4 1.2 fusion.30
  120.6 1.4 fusion.31
  122.0 0.1 copy.27
  122.2 0.1 maximum_convert_fusion
  122.3 0.4 fusion.25
  122.8 5.4 %collective-permute-start.2 = (bf16[16,1,256]{2,1,0:T(2,128)(2,1)S(1)}, bf16[16,1,256]{2,1,0:T(2,128)(2,1)S(1)}, u32[]{:S(2)}, u32[]{:S(2)}) collective-permute-start(bf16[16,1,256]{2,1,0:T(2,128)(2,1)S(1)} %get-tuple-element.25), channel_id=1, source_target_pairs={{0,1},{1,2},{2,3},{3,4},{4,5},{5,6},{6,7},{7,8},{8,9},{9,10},{10,1... | collective-permute-start | bytes 24584 | tf_op jit(solution)/shard_map/ppermute | solution.py:27
  128.1 0.2 fusion.28
  128.3 0.8 fusion.29
  129.2 7.8 %collective-permute-done.3 = bf16[16,1,256]{2,1,0:T(2,128)(2,1)S(1)} collective-permute-done((bf16[16,1,256]{2,1,0:T(2,128)(2,1)S(1)}, bf16[16,1,256]{2,1,0:T(2,128)(2,1)S(1)}, u32[]{:S(2)}, u32[]{:S(2)}) %collective-permute-start.3) | collective-permute-done | bytes 8224 | tf_op jit(solution)/shard_map/ppermute | solution.py:29
  137.0 0.1 maximum_convert_fusion.1
  137.2 6.6 %gather_fusion.1 = bf16[256,16,128]{2,1,0:T(8,128)(2,1)S(1)} fusion(bf16[16,4096,128]{2,0,1:T(8,128)(2,1)} %all-gather.3.cloned.1.call-done, s32[1024]{0:T(1024)S(1)} %pad_clamp_fusion), kind=kCustom, calls=%fused_computation.1 | custom fusion | bytes 2098176 | tf_op jit(solution)/shard_map/jit(_take)/gather | solution.py:50
  143.8 4.7 %fusion.2 = f32[16,64,128]{2,0,1:T(8,128)S(1)} fusion(bf16[1,64,4,128,128]{4,3,2,1,0:T(8,128)(2,1)} %param.8, bf16[16,64,4,128]{3,0,2,1:T(8,128)(2,1)S(1)} %bitcast.53, pred[64,4]{1,0:T(8,128)(4,1)S(1)} %copy.27), kind=kOutput, calls=%fused_computation.4 | convolution fusion | flops 134742016 | bytes 9961728 | tf_op jit(solution)/shard_map/vbkc,bkdc->vbd/dot_general | solution.py:52
  148.5 0.2 copy.29
  148.7 0.1 reshape.169
  148.8 0.9 broadcast_in_dim_reshape.3
  149.8 2.2 %fusion.10 = f32[1,16,32,256]{3,2,1,0:T(8,128)} fusion(f32[16,32,256]{2,1,0:T(8,128)S(1)} %get-tuple-element.14, f32[16,34,256]{2,1,0:T(8,128)S(1)} %maximum_convert_fusion.1, f32[16,32,255]{2,1,0:T(8,128)S(1)} %get-tuple-element.18, f32[16,32,1]{2,1,0:T(8,128)} %get-tuple-element.20, f32[16,32,1]{2,1,0:T(8,128)S(1)} %get-tuple-element.19, ...), kind=kLoop, calls=%fused_computation.12 | loop fusion | flops 1703936 | bytes 3702912 | tf_op jit(solution)/shard_map/broadcast_in_dim | solution.py:67
  (20 shorter events, 0.2 us)
Async XLA Ops:
  7.2 115.1 %copy-start = (f32[1,16,32,256]{3,2,1,0:T(8,128)S(1)}, f32[1,16,32,256]{3,2,1,0:T(8,128)}, u32[]{:S(2)}) copy-start(f32[1,16,32,256]{3,2,1,0:T(8,128)} %param.7) | copy-start | bytes 1572868
  7.2 115.1 %copy-start.2 = (f32[1,16]{1,0:T(1,128)S(1)}, f32[1,16]{1,0:T(1,128)}, u32[]{:S(2)}) copy-start(f32[1,16]{1,0:T(1,128)} %param.11) | copy-start | bytes 196
  7.2 130.0 %all-gather.3.cloned.1.call-start = ((), (), s32[]{:S(2)}) async-start(), calls=%async_computation | async-start | bytes 17039360 | tf_op jit(solution)/shard_map/all_gather | solution.py:45
  8.7 7.6 %collective-permute-start.4 = (bf16[16,64,128]{2,1,0:T(8,128)(2,1)S(1)}, bf16[16,64,128]{2,1,0:T(8,128)(2,1)S(1)}, u32[]{:S(2)}, u32[]{:S(2)}) collective-permute-start(bf16[16,64,128]{2,1,0:T(8,128)(2,1)S(1)} %convert_element_type.28), channel_id=1, source_target_pairs={{0,64},{64,0},{1,65},{65,1},{2,66},{66,2},{3,67},{67,3},{4,68},{68... | collective-permute-start | bytes 786440 | tf_op jit(solution)/shard_map/ppermute | solution.py:17
  17.2 104.9 %collective-permute-start = (bf16[16,1,256]{2,1,0:T(2,128)(2,1)S(1)}, bf16[16,1,256]{2,1,0:T(2,128)(2,1)S(1)}, u32[]{:S(2)}, u32[]{:S(2)}) collective-permute-start(bf16[16,1,256]{2,1,0:T(2,128)(2,1)S(1)} %get-tuple-element.27), channel_id=1, source_target_pairs={{0,1},{1,2},{2,3},{3,4},{4,5},{5,6},{6,7},{7,8},{8,9},{9,10},{10,1... | collective-permute-start | bytes 24584 | tf_op jit(solution)/shard_map/ppermute | solution.py:27
  21.5 100.6 %collective-permute-start.1 = (bf16[16,1,256]{2,1,0:T(2,128)(2,1)S(1)}, bf16[16,1,256]{2,1,0:T(2,128)(2,1)S(1)}, u32[]{:S(2)}, u32[]{:S(2)}) collective-permute-start(bf16[16,1,256]{2,1,0:T(2,128)(2,1)S(1)} %get-tuple-element.28), channel_id=1, source_target_pairs={{1,0},{2,1},{3,2},{4,3},{5,4},{6,5},{7,6},{8,7},{9,8},{10,9},{11,1... | collective-permute-start | bytes 24584 | tf_op jit(solution)/shard_map/ppermute | solution.py:29
  119.4 17.7 %copy-start.1 = (f32[32,256]{1,0:T(8,128)}, f32[32,256]{1,0:T(8,128)S(1)}, u32[]{:S(2)}) copy-start(f32[32,256]{1,0:T(8,128)S(1)} %convert_select_fusion) | copy-start | bytes 98308
  122.8 6.4 %collective-permute-start.2 = (bf16[16,1,256]{2,1,0:T(2,128)(2,1)S(1)}, bf16[16,1,256]{2,1,0:T(2,128)(2,1)S(1)}, u32[]{:S(2)}, u32[]{:S(2)}) collective-permute-start(bf16[16,1,256]{2,1,0:T(2,128)(2,1)S(1)} %get-tuple-element.25), channel_id=1, source_target_pairs={{0,1},{1,2},{2,3},{3,4},{4,5},{5,6},{6,7},{7,8},{8,9},{9,10},{10,1... | collective-permute-start | bytes 24584 | tf_op jit(solution)/shard_map/ppermute | solution.py:27
  128.1 8.9 %collective-permute-start.3 = (bf16[16,1,256]{2,1,0:T(2,128)(2,1)S(1)}, bf16[16,1,256]{2,1,0:T(2,128)(2,1)S(1)}, u32[]{:S(2)}, u32[]{:S(2)}) collective-permute-start(bf16[16,1,256]{2,1,0:T(2,128)(2,1)S(1)} %get-tuple-element.26), channel_id=1, source_target_pairs={{1,0},{2,1},{3,2},{4,3},{5,4},{6,5},{7,6},{8,7},{9,8},{10,9},{11,1... | collective-permute-start | bytes 24584 | tf_op jit(solution)/shard_map/ppermute | solution.py:29
Sparse Core Ops, SparseCore 0:
  17.3 107.7 all-gather.2
where the time goes:
time: 159 us
  blocking collectives  92 us (58%)
  local copies, waits for them, and re-layouts  15.8 us (10%)
  between operations  14.2 us (9%)
  waiting for transfers between devices  13.8 us (9%)
  starting transfers between devices  11.4 us (7%)
  other arithmetic  6.88 us (4%)
  matrix products  4.71 us (3%)
    all_gather x1, blocking collectives, per_device(): lax.all_gather(send_slots[0], 'tile', axis=0, tiled=True)  92 us
    ppermute x2, starting transfers between devices, with_halo(): lax.ppermute(tail, axis, [(i, (i + 1) % count) for i in range(count)])  9.66 us
    ppermute x2, waiting for transfers between devices, with_halo(): lax.ppermute(head, axis, [((i + 1) % count, i) for i in range(count)])  7.83 us
    gather x1, local copies, waits for them, and re-layouts, per_device(): picked = jnp.take(blocks, source, axis=1)  6.62 us
    ppermute x1, waiting for transfers between devices, partner(): return lax.ppermute(value, axis, pairs)  5.91 us
    dot_general x1, matrix products, per_device(): jnp.einsum('vbkc,bkdc->vbd', picked, weights[0], preferred_element_type=j...  4.71 us
  transfers between devices with their start and end apart: 6, of which 2 were waited for; matrix products, arithmetic and copies ran while one was open for 6% of the time, Pallas kernels for 0%

commit v1 on v0

v1 whole, which is shorter than its diff:
```python
import functools

import jax
import jax.numpy as jnp
from jax import lax
from jax.experimental import pallas as pl
from jax.experimental.pallas import tpu as pltpu
from jax.sharding import PartitionSpec as P

BLOCK = 128
MESH = pl.DeviceIdType.MESH


def target_tile(me, step, tiles):
    if tiles != 64:
        return lax.rem(me + step, tiles)
    core = (me % 2 + step % 2) % 2
    z_hi = (me // 32 + step // 2) % 2
    x = (me // 8 % 4 + step // 4) % 4
    y = (me // 2 % 4 + step // 16) % 4
    return z_hi * 32 + x * 8 + y * 2 + core


def kernel(
    tiles, slots, fields, rows, columns, blocks, sources,
    state_hbm, weights_hbm, lists_hbm, pos_hbm, diffusion_hbm, coupling_hbm, mask_hbm,
    new_ref, flux_ref,
    lists_ref, pos_ref, diffusion_ref, coupling_ref, mask_ref, cells, weights, surface, lists_v, lists_s, outbox, inbox, cover, edge, halo, side, stepped, flux,
    small_sem, state_sem, weights_sem, lists_sem, edge_send, edge_recv, list_send, list_recv, box_send, box_recv,
):
    comp, me = lax.axis_index("comp"), lax.axis_index("tile")
    other = 1 - comp
    above, below = (me + tiles - 1) % tiles, (me + 1) % tiles
    halves = columns // BLOCK

    load_state = [
        pltpu.make_async_copy(
            state_hbm.at[:, pl.ds(half * BLOCK, BLOCK)], cells.at[half], state_sem.at[half]
        )
        for half in range(halves)
    ]
    for copy in load_state:
        copy.start()
    load_small = [
        pltpu.make_async_copy(source, target, small_sem.at[number])
        for number, (source, target) in enumerate((
            (lists_hbm, lists_ref), (pos_hbm, pos_ref), (diffusion_hbm, diffusion_ref),
            (coupling_hbm, coupling_ref), (mask_hbm, mask_ref),
        ))
    ]
    for copy in load_small:
        copy.start()
    load_weights = pltpu.make_async_copy(weights_hbm, weights, weights_sem)
    load_weights.start()

    barrier = pltpu.get_barrier_semaphore()
    for neighbour in (above, below):
        pl.semaphore_signal(barrier, inc=1, device_id=(comp, neighbour), device_id_type=MESH)

    @pl.loop(0, tiles)
    def _(step):
        pl.semaphore_signal(
            barrier, inc=1, device_id=(other, target_tile(me, step, tiles)), device_id_type=MESH
        )

    for copy in load_small:
        copy.wait()
    cover[...] = jnp.where(comp == 1, mask_ref[...].astype(jnp.float32), 1.0)
    for copy in load_state:
        copy.wait()

    @pl.loop(0, rows)
    def _(row):
        for half in range(halves):
            picked = cells[half, pl.ds(row, fields, stride=rows)]
            surface[row * halves + half] = picked.astype(jnp.bfloat16)

    def whole(ref, here):
        return jnp.concatenate([ref[half, here] for half in range(halves)], axis=1)

    def line(row):
        return whole(cells, pl.ds(row, fields, stride=rows))

    edge[0, 0:fields] = line(0)
    edge[0, fields:2 * fields] = line(1)
    edge[0, 2 * fields:] = jnp.broadcast_to(cover[0:1], (8, columns))
    edge[1, 0:fields] = line(rows - 1)
    edge[1, fields:2 * fields] = line(rows - 2)
    edge[1, 2 * fields:] = jnp.broadcast_to(cover[rows - 1:rows], (8, columns))

    pl.semaphore_wait(barrier, tiles + 2)

    send_lists = pltpu.make_async_remote_copy(
        src_ref=lists_ref, dst_ref=lists_v, send_sem=list_send, recv_sem=list_recv,
        device_id=(other, me), device_id_type=MESH,
    )
    send_lists.start()
    send_edges = [
        pltpu.make_async_remote_copy(
            src_ref=edge.at[end], dst_ref=halo.at[end], send_sem=edge_send.at[end],
            recv_sem=edge_recv.at[end], device_id=(comp, neighbour), device_id_type=MESH,
        )
        for end, neighbour in ((0, above), (1, below))
    ]
    for copy in send_edges:
        copy.start()
    send_lists.wait()
    move_lists = pltpu.make_async_copy(lists_v, lists_s, lists_sem)
    move_lists.start()
    move_lists.wait()

    @pl.loop(0, tiles)
    def _(step):
        tile = target_tile(me, step, tiles)
        for slot in range(slots):
            outbox[tile, slot] = surface[lists_s[slot, tile]]
        pltpu.make_async_remote_copy(
            src_ref=outbox.at[tile], dst_ref=inbox.at[pl.ds(me * slots, slots)],
            send_sem=box_send, recv_sem=box_recv,
            device_id=(other, tile), device_id_type=MESH,
        ).start()

    for copy in send_edges:
        copy.wait()
    number = lax.broadcasted_iota(jnp.int32, (fields, columns), 0)
    rates = jnp.zeros((fields, columns), jnp.float32)
    for field in range(fields):
        rates = jnp.where(number == field, diffusion_ref[0, field], rates)

    def across(value):
        return pltpu.roll(value, 1, 1) + pltpu.roll(value, columns - 1, 1)

    for end, row in ((1, 0), (0, rows - 1)):
        near, far = halo[end, 0:fields], halo[end, fields:2 * fields]
        total = far + line(row) + across(near) - 4.0 * near
        side[end] = near + rates * halo[end, 2 * fields:2 * fields + 1] * total

    row_number = lax.broadcasted_iota(jnp.int32, (rows, columns), 0)

    def substep(value, first, last, rate):
        up = jnp.where(row_number == 0, first, pltpu.roll(value, 1, 0))
        down = jnp.where(row_number == rows - 1, last, pltpu.roll(value, rows - 1, 0))
        total = up + down + across(value) - 4.0 * value
        return value + rate * cover[...] * total

    @pl.loop(0, fields)
    def _(field):
        here = pl.ds(pl.multiple_of(field * rows, rows), rows)
        rate = diffusion_ref[0, field]
        value = whole(cells, here)
        value = substep(value, halo[1, pl.ds(field, 1)], halo[0, pl.ds(field, 1)], rate)
        value = substep(value, side[1, pl.ds(field, 1)], side[0, pl.ds(field, 1)], rate)
        stepped[here] = value

    load_weights.wait()
    pltpu.make_async_copy(inbox, inbox, box_recv).wait()

    @pl.loop(0, blocks // halves)
    def _(row):
        for half in range(halves):
            block = row * halves + half
            total = jnp.zeros((fields, BLOCK), jnp.float32)
            for source in range(sources):
                total += lax.dot_general(
                    inbox[pos_ref[source, block]], weights[block, source],
                    (((1,), (1,)), ((), ())), preferred_element_type=jnp.float32,
                )
            flux[half, pl.ds(row, fields, stride=rows)] = total

    @pl.loop(0, fields)
    def _(field):
        here = pl.ds(pl.multiple_of(field * rows, rows), rows)
        arrived = whole(flux, here)
        flux_ref[here] = arrived
        new_ref[here] = stepped[here] + coupling_ref[0, field] * cover[...] * arrived

    pltpu.make_async_copy(outbox, outbox, box_send).wait()


def per_device(tiles, state, weights, send_slots, recv_pos, diffusion, coupling, sea_mask):
    _, fields, rows, columns = state.shape
    blocks, sources = recv_pos.shape[1:]
    slots = send_slots.shape[3]
    lists = send_slots[0, 0].T
    positions = recv_pos[0].T
    flat = jax.ShapeDtypeStruct((fields * rows, columns), jnp.float32)
    vmem, hbm = pl.BlockSpec(memory_space=pltpu.VMEM), pl.BlockSpec(memory_space=pltpu.HBM)
    edge_rows = 2 * fields + 8
    dma = pltpu.SemaphoreType.DMA
    new, flux = pl.pallas_call(
        functools.partial(kernel, tiles, slots, fields, rows, columns, blocks, sources),
        out_shape=(flat, flat),
        in_specs=[hbm] * 7,
        out_specs=(vmem, vmem),
        scratch_shapes=[
            pltpu.VMEM((slots, tiles), jnp.int32),
            pltpu.SMEM((sources, blocks), jnp.int32),
            pltpu.SMEM((1, fields), jnp.float32),
            pltpu.SMEM((1, fields), jnp.float32),
            pltpu.VMEM((rows, columns), jnp.int32),
            pltpu.VMEM((columns // BLOCK, fields * rows, BLOCK), jnp.float32),
            pltpu.VMEM((blocks, sources, BLOCK, BLOCK), jnp.bfloat16),
            pltpu.VMEM((blocks, fields, BLOCK), jnp.bfloat16),
            pltpu.VMEM((slots, tiles), jnp.int32),
            pltpu.SMEM((slots, tiles), jnp.int32),
            pltpu.VMEM((tiles, slots, fields, BLOCK), jnp.bfloat16),
            pltpu.VMEM((tiles * slots, fields, BLOCK), jnp.bfloat16),
            pltpu.VMEM((rows, columns), jnp.float32),
            pltpu.VMEM((2, edge_rows, columns), jnp.float32),
            pltpu.VMEM((2, edge_rows, columns), jnp.float32),
            pltpu.VMEM((2, fields, columns), jnp.float32),
            pltpu.VMEM((fields * rows, columns), jnp.float32),
            pltpu.VMEM((columns // BLOCK, fields * rows, BLOCK), jnp.float32),
            dma((5,)), dma((columns // BLOCK,)), dma, dma, dma((2,)), dma((2,)), dma, dma, dma, dma,
        ],
        compiler_params=pltpu.CompilerParams(
            collective_id=0, has_side_effects=True, vmem_limit_bytes=60 * 2**20
        ),
    )(state.reshape(fields * rows, columns), weights[0], lists, positions, diffusion, coupling, sea_mask)
    return new.reshape(state.shape), flux.reshape(state.shape)


def solution(mesh):
    return jax.shard_map(
        functools.partial(per_device, mesh.shape["tile"]),
        mesh=mesh,
        in_specs=(
            P("comp", None, "tile", None),
            P("comp", "tile", None, None, None),
            P("comp", "tile", None, None),
            P("comp", "tile", None),
            P("comp", None),
            P("comp", None),
            P("tile", None),
        ),
        out_specs=(P("comp", None, "tile", None), P("comp", None, "tile", None)),
        check_vma=False,
    )
```

time: 159 us -> 61.3 us (0.39)
  the two profiles are of different devices: /device:TPU:31 before, /device:TPU:1 now
where the time goes in v1:
time: 61.3 us; the launch traced here: 61 us
  Pallas kernels  56.5 us (92%)
  local copies, waits for them, and re-layouts  3.76 us (6%)
  between operations  0.64 us (1%)
    pallas_call x1, Pallas kernels, per_device(): pl.pallas_call(functools.partial(kernel, tiles, slots, fields, rows, colu...  56.5 us
    unnamed x2, local copies, waits for them, and re-layouts  3.76 us

profile of v1, /device:TPU:1, one launch (start us, length us, event | category | flops | bytes accessed | tf_op | source)
XLA Modules:
  0.0 61.0 jit_solution(16054294590667609062)
XLA Ops:
  0.6 56.5 %shard_map.86 = (f32[512,256]{1,0:T(8,128)}, f32[512,256]{1,0:T(8,128)}) custom-call(f32[512,256]{1,0:T(8,128)} %bitcast.11, bf16[64,4,128,128]{3,2,1,0:T(8,128)(2,1)} %bitcast.10, s32[8,64]{1,0:T(8,128)} %bitcast.14, s32[4,64]{1,0:T(4,128)} %bitcast.15, f32[1,16]{1,0:T(1,128)} %diffusion_hbm.1, f32[1,16]{1,0:T(1,128)} %coupling_hbm.1, s32[32,256]{1,0:T(8,128)} %mask_hbm.1), custom_call_target="tpu_custom_call" | custom-call | tf_op jit(solution)/shard_map/pallas_call | solution.py:190
  57.2 1.9 %copy.11 = f32[1,16,32,256]{3,2,1,0:T(8,128)} copy(f32[1,16,32,256]{3,2,1,0:T(8,128)} %bitcast.13) | data formatting | bytes 1048576
  59.1 1.9 %copy.12 = f32[1,16,32,256]{3,2,1,0:T(8,128)} copy(f32[1,16,32,256]{3,2,1,0:T(8,128)} %bitcast.12) | data formatting | bytes 1048576

commit v2 on v1

--- a/solution.py
+++ b/solution.py
@@ -14,19 +14,17 @@
 def target_tile(me, step, tiles):
     if tiles != 64:
         return lax.rem(me + step, tiles)
-    core = (me % 2 + step % 2) % 2
-    z_hi = (me // 32 + step // 2) % 2
-    x = (me // 8 % 4 + step // 4) % 4
-    y = (me // 2 % 4 + step // 16) % 4
-    return z_hi * 32 + x * 8 + y * 2 + core
+    x, turn, part = step % 4, step // 4 % 4, step // 16
+    y, z_hi, core = (x + turn) % 4, (x + part) % 2, part // 2
+    return me ^ (z_hi * 32 + x * 8 + y * 2 + core)
 
 
 def kernel(
     tiles, slots, fields, rows, columns, blocks, sources,
     state_hbm, weights_hbm, lists_hbm, pos_hbm, diffusion_hbm, coupling_hbm, mask_hbm,
     new_ref, flux_ref,
-    lists_ref, pos_ref, diffusion_ref, coupling_ref, mask_ref, cells, weights, surface, lists_v, lists_s, outbox, inbox, cover, edge, halo, side, stepped, flux,
-    small_sem, state_sem, weights_sem, lists_sem, edge_send, edge_recv, list_send, list_recv, box_send, box_recv,
+    pos_ref, diffusion_ref, coupling_ref, mask_ref, cells, weights, surface, lists, outbox, inbox, cover, edge, halo, side, stepped, flux,
+    small_sem, state_sem, weights_sem, edge_send, edge_recv, list_send, list_recv, box_send, box_recv,
 ):
     comp, me = lax.axis_index("comp"), lax.axis_index("tile")
     other = 1 - comp
@@ -44,7 +42,7 @@
     load_small = [
         pltpu.make_async_copy(source, target, small_sem.at[number])
         for number, (source, target) in enumerate((
-            (lists_hbm, lists_ref), (pos_hbm, pos_ref), (diffusion_hbm, diffusion_ref),
+            (pos_hbm, pos_ref), (diffusion_hbm, diffusion_ref),
             (coupling_hbm, coupling_ref), (mask_hbm, mask_ref),
         ))
     ]
@@ -91,7 +89,7 @@
     pl.semaphore_wait(barrier, tiles + 2)
 
     send_lists = pltpu.make_async_remote_copy(
-        src_ref=lists_ref, dst_ref=lists_v, send_sem=list_send, recv_sem=list_recv,
+        src_ref=lists_hbm, dst_ref=lists, send_sem=list_send, recv_sem=list_recv,
         device_id=(other, me), device_id_type=MESH,
     )
     send_lists.start()
@@ -105,15 +103,12 @@
     for copy in send_edges:
         copy.start()
     send_lists.wait()
-    move_lists = pltpu.make_async_copy(lists_v, lists_s, lists_sem)
-    move_lists.start()
-    move_lists.wait()
 
     @pl.loop(0, tiles)
     def _(step):
         tile = target_tile(me, step, tiles)
         for slot in range(slots):
-            outbox[tile, slot] = surface[lists_s[slot, tile]]
+            outbox[tile, slot] = surface[lists[slot, tile]]
         pltpu.make_async_remote_copy(
             src_ref=outbox.at[tile], dst_ref=inbox.at[pl.ds(me * slots, slots)],
             send_sem=box_send, recv_sem=box_recv,
@@ -155,17 +150,15 @@
     load_weights.wait()
     pltpu.make_async_copy(inbox, inbox, box_recv).wait()
 
-    @pl.loop(0, blocks // halves)
+    @pl.loop(0, blocks // halves, unroll=8)
     def _(row):
         for half in range(halves):
             block = row * halves + half
-            total = jnp.zeros((fields, BLOCK), jnp.float32)
-            for source in range(sources):
-                total += lax.dot_general(
-                    inbox[pos_ref[source, block]], weights[block, source],
-                    (((1,), (1,)), ((), ())), preferred_element_type=jnp.float32,
-                )
-            flux[half, pl.ds(row, fields, stride=rows)] = total
+            picked = jnp.concatenate([inbox[pos_ref[source, block]] for source in range(sources)], axis=1)
+            weight = jnp.concatenate([weights[block, source] for source in range(sources)], axis=1)
+            flux[half, pl.ds(row, fields, stride=rows)] = lax.dot_general(
+                picked, weight, (((1,), (1,)), ((), ())), preferred_element_type=jnp.float32,
+            )
 
     @pl.loop(0, fields)
     def _(field):
@@ -181,8 +174,6 @@
     _, fields, rows, columns = state.shape
     blocks, sources = recv_pos.shape[1:]
     slots = send_slots.shape[3]
-    lists = send_slots[0, 0].T
-    positions = recv_pos[0].T
     flat = jax.ShapeDtypeStruct((fields * rows, columns), jnp.float32)
     vmem, hbm = pl.BlockSpec(memory_space=pltpu.VMEM), pl.BlockSpec(memory_space=pltpu.HBM)
     edge_rows = 2 * fields + 8
@@ -193,7 +184,6 @@
         in_specs=[hbm] * 7,
         out_specs=(vmem, vmem),
         scratch_shapes=[
-            pltpu.VMEM((slots, tiles), jnp.int32),
             pltpu.SMEM((sources, blocks), jnp.int32),
             pltpu.SMEM((1, fields), jnp.float32),
             pltpu.SMEM((1, fields), jnp.float32),
@@ -201,7 +191,6 @@
             pltpu.VMEM((columns // BLOCK, fields * rows, BLOCK), jnp.float32),
             pltpu.VMEM((blocks, sources, BLOCK, BLOCK), jnp.bfloat16),
             pltpu.VMEM((blocks, fields, BLOCK), jnp.bfloat16),
-            pltpu.VMEM((slots, tiles), jnp.int32),
             pltpu.SMEM((slots, tiles), jnp.int32),
             pltpu.VMEM((tiles, slots, fields, BLOCK), jnp.bfloat16),
             pltpu.VMEM((tiles * slots, fields, BLOCK), jnp.bfloat16),
@@ -211,12 +200,14 @@
             pltpu.VMEM((2, fields, columns), jnp.float32),
             pltpu.VMEM((fields * rows, columns), jnp.float32),
             pltpu.VMEM((columns // BLOCK, fields * rows, BLOCK), jnp.float32),
-            dma((5,)), dma((columns // BLOCK,)), dma, dma, dma((2,)), dma((2,)), dma, dma, dma, dma,
+            dma((4,)), dma((columns // BLOCK,)), dma, dma((2,)), dma((2,)), dma, dma, dma, dma,
         ],
         compiler_params=pltpu.CompilerParams(
-            collective_id=0, has_side_effects=True, vmem_limit_bytes=60 * 2**20
+            collective_id=0, has_side_effects=True, vmem_limit_bytes=32 * 2**20
         ),
-    )(state.reshape(fields * rows, columns), weights[0], lists, positions, diffusion, coupling, sea_mask)
+    )(*(pltpu.with_memory_space_constraint(value, pltpu.HBM) for value in (
+        state.reshape(fields * rows, columns), weights[0], send_slots[0, 0].T, recv_pos[0].T, diffusion, coupling, sea_mask
+    )))
     return new.reshape(state.shape), flux.reshape(state.shape)
 
 

time: 61.3 us -> 45.5 us (0.74)
  Pallas kernels: 56.5 us -> 43.2 us
  local copies, waits for them, and re-layouts: 3.76 us -> 1.59 us
    pallas_call x1, Pallas kernels: 56.5 us -> 43.2 us  [per_device(): pl.pallas_call(functools.partial(kernel, tiles, slots, fields, rows, colu...]
    unnamed x2, local copies, waits for them, and re-layouts: 3.76 us -> 1.59 us
where the time goes in v2:
time: 45.5 us; the launch traced here: 45.4 us
  Pallas kernels  43.2 us (95%)
  local copies, waits for them, and re-layouts  1.59 us (3%)
  between operations  0.64 us (1%)
    pallas_call x1, Pallas kernels, per_device(): pl.pallas_call(functools.partial(kernel, tiles, slots, fields, rows, colu...  43.2 us
    unnamed x2, local copies, waits for them, and re-layouts  1.59 us

profile of v2, /device:TPU:1, one launch (start us, length us, event | category | flops | bytes accessed | tf_op | source)
XLA Modules:
  0.0 45.4 jit_solution(12245310175024801166)
XLA Ops:
  0.6 43.2 %shard_map.86 = (f32[512,256]{1,0:T(8,128)S(1)}, f32[512,256]{1,0:T(8,128)S(1)}) custom-call(f32[512,256]{1,0:T(8,128)} %bitcast.13, bf16[64,4,128,128]{3,2,1,0:T(8,128)(2,1)} %bitcast.12, s32[8,64]{1,0:T(8,128)} %bitcast.14, s32[4,64]{1,0:T(4,128)} %bitcast.15, f32[1,16]{1,0:T(1,128)} %diffusion_hbm.1, f32[1,16]{1,0:T(1,128)} %coupling_hbm.1, ...), custom_call_target="tpu_custom_call" | custom-call | tf_op jit(solution)/shard_map/pallas_call | solution.py:181
  43.8 0.8 %copy.11 = f32[1,16,32,256]{3,2,1,0:T(8,128)} copy(f32[1,16,32,256]{3,2,1,0:T(8,128)S(1)} %bitcast.11) | data formatting | bytes 1048576
  44.6 0.8 %copy.12 = f32[1,16,32,256]{3,2,1,0:T(8,128)} copy(f32[1,16,32,256]{3,2,1,0:T(8,128)S(1)} %bitcast.10) | data formatting | bytes 1048576

commit v3 on v2

--- a/solution.py
+++ b/solution.py
@@ -8,6 +8,8 @@
 from jax.sharding import PartitionSpec as P
 
 BLOCK = 128
+GROUP = 4
+GROUP_ROWS = 8
 MESH = pl.DeviceIdType.MESH
 
 
@@ -19,12 +21,12 @@
     return me ^ (z_hi * 32 + x * 8 + y * 2 + core)
 
 
-def kernel(
+def exchange(
     tiles, slots, fields, rows, columns, blocks, sources,
     state_hbm, weights_hbm, lists_hbm, pos_hbm, diffusion_hbm, coupling_hbm, mask_hbm,
-    new_ref, flux_ref,
-    pos_ref, diffusion_ref, coupling_ref, mask_ref, cells, weights, surface, lists, outbox, inbox, cover, edge, halo, side, stepped, flux,
-    small_sem, state_sem, weights_sem, edge_send, edge_recv, list_send, list_recv, box_send, box_recv,
+    products, stepped, cover, gains, pos_ref,
+    diffusion_ref, coupling_ref, mask_ref, cells, weights, surface, lists, outbox, inbox, edge, halo, side, users_v, users,
+    small_sem, state_sem, weights_sem, users_sem, edge_send, edge_recv, list_send, list_recv, box_send, box_recv,
 ):
     comp, me = lax.axis_index("comp"), lax.axis_index("tile")
     other = 1 - comp
@@ -55,7 +57,7 @@
     for neighbour in (above, below):
         pl.semaphore_signal(barrier, inc=1, device_id=(comp, neighbour), device_id_type=MESH)
 
-    @pl.loop(0, tiles)
+    @pl.loop(0, tiles, unroll=tiles)
     def _(step):
         pl.semaphore_signal(
             barrier, inc=1, device_id=(other, target_tile(me, step, tiles)), device_id_type=MESH
@@ -104,23 +106,42 @@
         copy.start()
     send_lists.wait()
 
-    @pl.loop(0, tiles)
+    @pl.loop(0, tiles, unroll=tiles)
     def _(step):
         tile = target_tile(me, step, tiles)
         for slot in range(slots):
             outbox[tile, slot] = surface[lists[slot, tile]]
         pltpu.make_async_remote_copy(
             src_ref=outbox.at[tile], dst_ref=inbox.at[pl.ds(me * slots, slots)],
-            send_sem=box_send, recv_sem=box_recv,
+            send_sem=box_send, recv_sem=box_recv.at[me],
             device_id=(other, tile), device_id_type=MESH,
         ).start()
 
+    place = lax.broadcasted_iota(jnp.int32, (slots, tiles), 1) * slots + lax.broadcasted_iota(
+        jnp.int32, (slots, tiles), 0
+    )
+
+    def find(block, found):
+        for source in range(sources):
+            found = jnp.where(place == pos_ref[source, block], block * sources + source, found)
+        return found
+
+    users_v[...] = lax.fori_loop(0, blocks, find, jnp.zeros((slots, tiles), jnp.int32), unroll=8)
+    move_users = pltpu.make_async_copy(users_v, users, users_sem)
+    move_users.start()
+
     for copy in send_edges:
         copy.wait()
-    number = lax.broadcasted_iota(jnp.int32, (fields, columns), 0)
-    rates = jnp.zeros((fields, columns), jnp.float32)
-    for field in range(fields):
-        rates = jnp.where(number == field, diffusion_ref[0, field], rates)
+
+    def spread(ref, width):
+        number = lax.broadcasted_iota(jnp.int32, (fields, width), 0)
+        values = jnp.zeros((fields, width), jnp.float32)
+        for field in range(fields):
+            values = jnp.where(number == field, ref[0, field], values)
+        return values
+
+    rates = spread(diffusion_ref, columns)
+    gains[...] = spread(coupling_ref, BLOCK)
 
     def across(value):
         return pltpu.roll(value, 1, 1) + pltpu.roll(value, columns - 1, 1)
@@ -145,70 +166,129 @@
         value = whole(cells, here)
         value = substep(value, halo[1, pl.ds(field, 1)], halo[0, pl.ds(field, 1)], rate)
         value = substep(value, side[1, pl.ds(field, 1)], side[0, pl.ds(field, 1)], rate)
-        stepped[here] = value
-
+        for half in range(halves):
+            stepped[half, here] = value[:, half * BLOCK:(half + 1) * BLOCK]
+
+    move_users.wait()
     load_weights.wait()
-    pltpu.make_async_copy(inbox, inbox, box_recv).wait()
-
-    @pl.loop(0, blocks // halves, unroll=8)
-    def _(row):
-        for half in range(halves):
-            block = row * halves + half
-            picked = jnp.concatenate([inbox[pos_ref[source, block]] for source in range(sources)], axis=1)
-            weight = jnp.concatenate([weights[block, source] for source in range(sources)], axis=1)
-            flux[half, pl.ds(row, fields, stride=rows)] = lax.dot_general(
-                picked, weight, (((1,), (1,)), ((), ())), preferred_element_type=jnp.float32,
-            )
-
-    @pl.loop(0, fields)
-    def _(field):
-        here = pl.ds(pl.multiple_of(field * rows, rows), rows)
-        arrived = whole(flux, here)
-        flux_ref[here] = arrived
-        new_ref[here] = stepped[here] + coupling_ref[0, field] * cover[...] * arrived
+
+    @pl.loop(0, tiles // GROUP)
+    def _(group):
+        froms = [target_tile(me, group * GROUP + turn, tiles) for turn in range(GROUP)]
+        for tile in froms:
+            arrived = inbox.at[pl.ds(tile * slots, slots)]
+            pltpu.make_async_copy(arrived, arrived, box_recv.at[tile]).wait()
+        for tile in froms:
+            for slot in range(0, slots, 2):
+                first = tile * slots + slot
+                nothing = jnp.zeros((fields, BLOCK), jnp.bfloat16)
+                picked = jnp.concatenate([
+                    jnp.concatenate([inbox[first], nothing], axis=1),
+                    jnp.concatenate([nothing, inbox[first + 1]], axis=1),
+                ], axis=0)
+                weight = jnp.concatenate(
+                    [weights[users[slot, tile]], weights[users[slot + 1, tile]]], axis=1
+                )
+                pair = lax.dot_general(
+                    picked, weight, (((1,), (1,)), ((), ())), preferred_element_type=jnp.float32
+                )
+                products[first] = pair[:fields]
+                products[first + 1] = pair[fields:]
 
     pltpu.make_async_copy(outbox, outbox, box_send).wait()
+
+
+def finish(
+    fields, rows, columns, sources,
+    products, stepped, cover, gains, pos_ref, new_hbm, flux_hbm, new, flux, new_sem, flux_sem,
+):
+    halves = columns // BLOCK
+    copies = []
+    for group in range(rows // GROUP_ROWS):
+        for row in range(group * GROUP_ROWS, (group + 1) * GROUP_ROWS):
+            lines = pl.ds(row, fields, stride=rows)
+            for half in range(halves):
+                block = row * halves + half
+                total = products[pos_ref[0, block]]
+                for source in range(1, sources):
+                    total += products[pos_ref[source, block]]
+                flux[half, lines] = total
+                new[half, lines] = stepped[half, lines] + (
+                    gains[...] * cover[row:row + 1, half * BLOCK:(half + 1) * BLOCK] * total
+                )
+        here = pl.ds(group * GROUP_ROWS, GROUP_ROWS)
+        for number, (source, target, sem) in enumerate(((new, new_hbm, new_sem), (flux, flux_hbm, flux_sem))):
+            for half in range(halves):
+                copy = pltpu.make_async_copy(
+                    source.reshape(halves, fields, rows, BLOCK).at[half, :, here],
+                    target.at[:, here, pl.ds(half * BLOCK, BLOCK)],
+                    sem.at[group, half],
+                )
+                copy.start()
+                copies.append(copy)
+    for copy in copies:
+        copy.wait()
 
 
 def per_device(tiles, state, weights, send_slots, recv_pos, diffusion, coupling, sea_mask):
     _, fields, rows, columns = state.shape
     blocks, sources = recv_pos.shape[1:]
     slots = send_slots.shape[3]
-    flat = jax.ShapeDtypeStruct((fields * rows, columns), jnp.float32)
-    vmem, hbm = pl.BlockSpec(memory_space=pltpu.VMEM), pl.BlockSpec(memory_space=pltpu.HBM)
+    halves = columns // BLOCK
+    vmem, smem, hbm = (pl.BlockSpec(memory_space=m) for m in (pltpu.VMEM, pltpu.SMEM, pltpu.HBM))
     edge_rows = 2 * fields + 8
     dma = pltpu.SemaphoreType.DMA
-    new, flux = pl.pallas_call(
-        functools.partial(kernel, tiles, slots, fields, rows, columns, blocks, sources),
-        out_shape=(flat, flat),
+    operands = (
+        state.reshape(fields * rows, columns), weights.reshape(blocks * sources, BLOCK, BLOCK),
+        send_slots[0, 0].T, recv_pos[0].T, diffusion, coupling, sea_mask,
+    )
+    between = pl.pallas_call(
+        functools.partial(exchange, tiles, slots, fields, rows, columns, blocks, sources),
+        out_shape=(
+            pltpu.VMEM((tiles * slots, fields, BLOCK), jnp.float32),
+            pltpu.VMEM((halves, fields * rows, BLOCK), jnp.float32),
+            pltpu.VMEM((rows, columns), jnp.float32),
+            pltpu.VMEM((fields, BLOCK), jnp.float32),
+            pltpu.SMEM((sources, blocks), jnp.int32),
+        ),
         in_specs=[hbm] * 7,
-        out_specs=(vmem, vmem),
+        out_specs=(vmem, vmem, vmem, vmem, smem),
         scratch_shapes=[
-            pltpu.SMEM((sources, blocks), jnp.int32),
             pltpu.SMEM((1, fields), jnp.float32),
             pltpu.SMEM((1, fields), jnp.float32),
             pltpu.VMEM((rows, columns), jnp.int32),
-            pltpu.VMEM((columns // BLOCK, fields * rows, BLOCK), jnp.float32),
-            pltpu.VMEM((blocks, sources, BLOCK, BLOCK), jnp.bfloat16),
+            pltpu.VMEM((halves, fields * rows, BLOCK), jnp.float32),
+            pltpu.VMEM((blocks * sources, BLOCK, BLOCK), jnp.bfloat16),
             pltpu.VMEM((blocks, fields, BLOCK), jnp.bfloat16),
             pltpu.SMEM((slots, tiles), jnp.int32),
             pltpu.VMEM((tiles, slots, fields, BLOCK), jnp.bfloat16),
             pltpu.VMEM((tiles * slots, fields, BLOCK), jnp.bfloat16),
-            pltpu.VMEM((rows, columns), jnp.float32),
             pltpu.VMEM((2, edge_rows, columns), jnp.float32),
             pltpu.VMEM((2, edge_rows, columns), jnp.float32),
             pltpu.VMEM((2, fields, columns), jnp.float32),
-            pltpu.VMEM((fields * rows, columns), jnp.float32),
-            pltpu.VMEM((columns // BLOCK, fields * rows, BLOCK), jnp.float32),
-            dma((4,)), dma((columns // BLOCK,)), dma, dma((2,)), dma((2,)), dma, dma, dma, dma,
+            pltpu.VMEM((slots, tiles), jnp.int32),
+            pltpu.SMEM((slots, tiles), jnp.int32),
+            dma((4,)), dma((halves,)), dma, dma, dma((2,)), dma((2,)), dma, dma, dma, dma((tiles,)),
         ],
         compiler_params=pltpu.CompilerParams(
             collective_id=0, has_side_effects=True, vmem_limit_bytes=32 * 2**20
         ),
-    )(*(pltpu.with_memory_space_constraint(value, pltpu.HBM) for value in (
-        state.reshape(fields * rows, columns), weights[0], send_slots[0, 0].T, recv_pos[0].T, diffusion, coupling, sea_mask
-    )))
-    return new.reshape(state.shape), flux.reshape(state.shape)
+    )(*(pltpu.with_memory_space_constraint(value, pltpu.HBM) for value in operands))
+    result = jax.ShapeDtypeStruct((fields, rows, columns), jnp.float32)
+    groups = rows // GROUP_ROWS
+    new, flux = pl.pallas_call(
+        functools.partial(finish, fields, rows, columns, sources),
+        out_shape=(result, result),
+        in_specs=[vmem, vmem, vmem, vmem, smem],
+        out_specs=(hbm, hbm),
+        scratch_shapes=[
+            pltpu.VMEM((halves, fields * rows, BLOCK), jnp.float32),
+            pltpu.VMEM((halves, fields * rows, BLOCK), jnp.float32),
+            dma((groups, halves)), dma((groups, halves)),
+        ],
+        compiler_params=pltpu.CompilerParams(vmem_limit_bytes=32 * 2**20),
+    )(*between)
+    return new[None], flux[None]
 
 
 def solution(mesh):

time: 45.5 us -> 42.6 us (0.936)
  local copies, waits for them, and re-layouts: 1.59 us -> 0 us
  Pallas kernels: 43.2 us -> 41.9 us
    unnamed x2 -> x0, local copies, waits for them, and re-layouts: 1.59 us -> none
    pallas_call x1 -> x2, Pallas kernels: 43.2 us -> 41.9 us  [the longest x1 39.8 us: per_device(): pl.pallas_call(functools.partial(exchange, tiles, slots, fields, rows, co...]
where the time goes in v3:
time: 42.6 us; the launch traced here: 42.5 us
  Pallas kernels  41.9 us (98%)
  between operations  0.64 us (2%)
    pallas_call x1, Pallas kernels, per_device(): pl.pallas_call(functools.partial(exchange, tiles, slots, fields, rows, co...  39.8 us
    pallas_call x1, Pallas kernels, per_device(): pl.pallas_call(functools.partial(finish, fields, rows, columns, sources),...  2.11 us

profile of v3, /device:TPU:1, one launch (start us, length us, event | category | flops | bytes accessed | tf_op | source)
XLA Modules:
  0.0 42.5 jit_solution(9852719051345389570)
XLA Ops:
  0.6 39.8 %shard_map.86 = (f32[512,16,128]{2,1,0:T(8,128)S(1)}, f32[2,512,128]{2,1,0:T(8,128)S(1)}, f32[32,256]{1,0:T(8,128)S(1)}, f32[16,128]{1,0:T(8,128)S(1)}, s32[4,64]{1,0:T(4,128)S(4)}) custom-call(f32[512,256]{1,0:T(8,128)} %bitcast.11, bf16[256,128,128]{2,1,0:T(8,128)(2,1)} %bitcast.10, s32[8,64]{1,0:T(8,128)} %bitcast.12, s32[4,64]{1,0:T(4,128)} %bitcast.13, ...), custom_call_target="tpu_custom_call" | custom-call | tf_op jit(solution)/shard_map/pallas_call | solution.py:245
  40.4 2.1 %shard_map.87 = (f32[16,32,256]{2,1,0:T(8,128)}, f32[16,32,256]{2,1,0:T(8,128)}) custom-call(f32[512,16,128]{2,1,0:T(8,128)S(1)} %get-tuple-element.9.products, f32[2,512,128]{2,1,0:T(8,128)S(1)} %get-tuple-element.10.stepped, f32[32,256]{1,0:T(8,128)S(1)} %get-tuple-element.11.cover, f32[16,128]{1,0:T(8,128)S(1)} %get-tuple-element.12.gains, ...), custom_call_target="tpu_custom_call" | custom-call | tf_op jit(solution)/shard_map/pallas_call | solution.py:279

commit v4 on v3

--- a/solution.py
+++ b/solution.py
@@ -17,7 +17,7 @@
     if tiles != 64:
         return lax.rem(me + step, tiles)
     x, turn, part = step % 4, step // 4 % 4, step // 16
-    y, z_hi, core = (x + turn) % 4, (x + part) % 2, part // 2
+    y, z_hi, core = (x + turn) % 4, (x // 2 + turn + part) % 2, (part // 2 + x) % 2
     return me ^ (z_hi * 32 + x * 8 + y * 2 + core)
 
 

time: 42.6 us -> 42 us (0.986)
  Pallas kernels: 41.9 us -> 41.3 us
    pallas_call x1, Pallas kernels: 39.8 us -> 39.1 us  [per_device(): pl.pallas_call(functools.partial(exchange, tiles, slots, fields, rows, co...]
where the time goes in v4:
time: 42 us; the launch traced here: 41.9 us
  Pallas kernels  41.3 us (98%)
  between operations  0.64 us (2%)
    pallas_call x1, Pallas kernels, per_device(): pl.pallas_call(functools.partial(exchange, tiles, slots, fields, rows, co...  39.1 us
    pallas_call x1, Pallas kernels, per_device(): pl.pallas_call(functools.partial(finish, fields, rows, columns, sources),...  2.12 us

profile of v4, /device:TPU:1, one launch (start us, length us, event | category | flops | bytes accessed | tf_op | source)
XLA Modules:
  0.0 41.9 jit_solution(1117676960741084167)
XLA Ops:
  0.6 39.1 %shard_map.86 = (f32[512,16,128]{2,1,0:T(8,128)S(1)}, f32[2,512,128]{2,1,0:T(8,128)S(1)}, f32[32,256]{1,0:T(8,128)S(1)}, f32[16,128]{1,0:T(8,128)S(1)}, s32[4,64]{1,0:T(4,128)S(4)}) custom-call(f32[512,256]{1,0:T(8,128)} %bitcast.11, bf16[256,128,128]{2,1,0:T(8,128)(2,1)} %bitcast.10, s32[8,64]{1,0:T(8,128)} %bitcast.12, s32[4,64]{1,0:T(4,128)} %bitcast.13, ...), custom_call_target="tpu_custom_call" | custom-call | tf_op jit(solution)/shard_map/pallas_call | solution.py:245
  39.8 2.1 %shard_map.87 = (f32[16,32,256]{2,1,0:T(8,128)}, f32[16,32,256]{2,1,0:T(8,128)}) custom-call(f32[512,16,128]{2,1,0:T(8,128)S(1)} %get-tuple-element.9.products, f32[2,512,128]{2,1,0:T(8,128)S(1)} %get-tuple-element.10.stepped, f32[32,256]{1,0:T(8,128)S(1)} %get-tuple-element.11.cover, f32[16,128]{1,0:T(8,128)S(1)} %get-tuple-element.12.gains, ...), custom_call_target="tpu_custom_call" | custom-call | tf_op jit(solution)/shard_map/pallas_call | solution.py:279

commit v5 on v4

--- a/solution.py
+++ b/solution.py
@@ -24,8 +24,8 @@
 def exchange(
     tiles, slots, fields, rows, columns, blocks, sources,
     state_hbm, weights_hbm, lists_hbm, pos_hbm, diffusion_hbm, coupling_hbm, mask_hbm,
-    products, stepped, cover, gains, pos_ref,
-    diffusion_ref, coupling_ref, mask_ref, cells, weights, surface, lists, outbox, inbox, edge, halo, side, users_v, users,
+    products, stepped, cover, coupling_ref, pos_ref,
+    diffusion_ref, mask_ref, cells, weights, surface, lists, outbox, inbox, edge, halo, side, users_v, users,
     small_sem, state_sem, weights_sem, users_sem, edge_send, edge_recv, list_send, list_recv, box_send, box_recv,
 ):
     comp, me = lax.axis_index("comp"), lax.axis_index("tile")
@@ -133,15 +133,10 @@
     for copy in send_edges:
         copy.wait()
 
-    def spread(ref, width):
-        number = lax.broadcasted_iota(jnp.int32, (fields, width), 0)
-        values = jnp.zeros((fields, width), jnp.float32)
-        for field in range(fields):
-            values = jnp.where(number == field, ref[0, field], values)
-        return values
-
-    rates = spread(diffusion_ref, columns)
-    gains[...] = spread(coupling_ref, BLOCK)
+    number = lax.broadcasted_iota(jnp.int32, (fields, columns), 0)
+    rates = jnp.zeros((fields, columns), jnp.float32)
+    for field in range(fields):
+        rates = jnp.where(number == field, diffusion_ref[0, field], rates)
 
     def across(value):
         return pltpu.roll(value, 1, 1) + pltpu.roll(value, columns - 1, 1)
@@ -200,22 +195,28 @@
 
 def finish(
     fields, rows, columns, sources,
-    products, stepped, cover, gains, pos_ref, new_hbm, flux_hbm, new, flux, new_sem, flux_sem,
+    products, stepped, cover, coupling_ref, pos_ref, new_hbm, flux_hbm, new, flux, new_sem, flux_sem,
 ):
     halves = columns // BLOCK
     copies = []
     for group in range(rows // GROUP_ROWS):
-        for row in range(group * GROUP_ROWS, (group + 1) * GROUP_ROWS):
-            lines = pl.ds(row, fields, stride=rows)
-            for half in range(halves):
+        for half in range(halves):
+            totals = []
+            for row in range(group * GROUP_ROWS, (group + 1) * GROUP_ROWS):
                 block = row * halves + half
                 total = products[pos_ref[0, block]]
                 for source in range(1, sources):
                     total += products[pos_ref[source, block]]
-                flux[half, lines] = total
-                new[half, lines] = stepped[half, lines] + (
-                    gains[...] * cover[row:row + 1, half * BLOCK:(half + 1) * BLOCK] * total
-                )
+                totals.append(total)
+            turned = jnp.swapaxes(jnp.stack(totals), 0, 1)
+            for field in range(fields):
+                flux[half, pl.ds(field * rows + group * GROUP_ROWS, GROUP_ROWS)] = turned[field]
+        shares = cover[group * GROUP_ROWS:(group + 1) * GROUP_ROWS]
+        for field in range(fields):
+            lines = pl.ds(field * rows + group * GROUP_ROWS, GROUP_ROWS)
+            for half in range(halves):
+                share = coupling_ref[0, field] * shares[:, half * BLOCK:(half + 1) * BLOCK]
+                new[half, lines] = stepped[half, lines] + share * flux[half, lines]
         here = pl.ds(group * GROUP_ROWS, GROUP_ROWS)
         for number, (source, target, sem) in enumerate(((new, new_hbm, new_sem), (flux, flux_hbm, flux_sem))):
             for half in range(halves):
@@ -248,13 +249,12 @@
             pltpu.VMEM((tiles * slots, fields, BLOCK), jnp.float32),
             pltpu.VMEM((halves, fields * rows, BLOCK), jnp.float32),
             pltpu.VMEM((rows, columns), jnp.float32),
-            pltpu.VMEM((fields, BLOCK), jnp.float32),
+            pltpu.SMEM((1, fields), jnp.float32),
             pltpu.SMEM((sources, blocks), jnp.int32),
         ),
         in_specs=[hbm] * 7,
-        out_specs=(vmem, vmem, vmem, vmem, smem),
+        out_specs=(vmem, vmem, vmem, smem, smem),
         scratch_shapes=[
-            pltpu.SMEM((1, fields), jnp.float32),
             pltpu.SMEM((1, fields), jnp.float32),
             pltpu.VMEM((rows, columns), jnp.int32),
             pltpu.VMEM((halves, fields * rows, BLOCK), jnp.float32),
@@ -279,7 +279,7 @@
     new, flux = pl.pallas_call(
         functools.partial(finish, fields, rows, columns, sources),
         out_shape=(result, result),
-        in_specs=[vmem, vmem, vmem, vmem, smem],
+        in_specs=[vmem, vmem, vmem, smem, smem],
         out_specs=(hbm, hbm),
         scratch_shapes=[
             pltpu.VMEM((halves, fields * rows, BLOCK), jnp.float32),

time: 42 us -> 41.2 us (0.981)
  Pallas kernels: 41.3 us -> 40.4 us
    pallas_call x1, Pallas kernels: 2.12 us -> 1.28 us  [per_device(): pl.pallas_call(functools.partial(finish, fields, rows, columns, sources),...]
where the time goes in v5:
time: 41.2 us; the launch traced here: 41.1 us
  Pallas kernels  40.4 us (98%)
  between operations  0.64 us (2%)
    pallas_call x1, Pallas kernels, per_device(): pl.pallas_call(functools.partial(exchange, tiles, slots, fields, rows, co...  39.1 us
    pallas_call x1, Pallas kernels, per_device(): pl.pallas_call(functools.partial(finish, fields, rows, columns, sources),...  1.28 us

profile of v5, /device:TPU:1, one launch (start us, length us, event | category | flops | bytes accessed | tf_op | source)
XLA Modules:
  0.0 41.1 jit_solution(8547534616563932907)
XLA Ops:
  0.6 39.1 %shard_map.86 = (f32[512,16,128]{2,1,0:T(8,128)S(1)}, f32[2,512,128]{2,1,0:T(8,128)S(1)}, f32[32,256]{1,0:T(8,128)S(1)}, f32[1,16]{1,0:T(1,128)S(4)}, s32[4,64]{1,0:T(4,128)S(4)}) custom-call(f32[512,256]{1,0:T(8,128)} %bitcast.11, bf16[256,128,128]{2,1,0:T(8,128)(2,1)} %bitcast.10, s32[8,64]{1,0:T(8,128)} %bitcast.12, s32[4,64]{1,0:T(4,128)} %bitcast.13, ...), custom_call_target="tpu_custom_call" | custom-call | tf_op jit(solution)/shard_map/pallas_call | solution.py:246
  39.8 1.3 %shard_map.87 = (f32[16,32,256]{2,1,0:T(8,128)}, f32[16,32,256]{2,1,0:T(8,128)}) custom-call(f32[512,16,128]{2,1,0:T(8,128)S(1)} %get-tuple-element.9.products, f32[2,512,128]{2,1,0:T(8,128)S(1)} %get-tuple-element.10.stepped, f32[32,256]{1,0:T(8,128)S(1)} %get-tuple-element.11.cover, f32[1,16]{1,0:T(1,128)S(4)} %get-tuple-element.12.coupling_ref, ...), custom_call_target="tpu_custom_call" | custom-call | tf_op jit(solution)/shard_map/pallas_call | solution.py:279

commit v6 on v5

--- a/solution.py
+++ b/solution.py
@@ -17,7 +17,7 @@
     if tiles != 64:
         return lax.rem(me + step, tiles)
     x, turn, part = step % 4, step // 4 % 4, step // 16
-    y, z_hi, core = (x + turn) % 4, (x // 2 + turn + part) % 2, (part // 2 + x) % 2
+    y, z_hi, core = (x + turn) % 4, (x + turn + part) % 2, (part // 2 + x // 2) % 2
     return me ^ (z_hi * 32 + x * 8 + y * 2 + core)
 
 

time: 41.2 us -> 40.8 us (level)
  Pallas kernels: 40.4 us -> 39.8 us
    pallas_call x1, Pallas kernels: 39.1 us -> 38.5 us  [per_device(): pl.pallas_call(functools.partial(exchange, tiles, slots, fields, rows, co...]
where the time goes in v6:
time: 40.8 us; the launch traced here: 40.5 us
  Pallas kernels  39.8 us (98%)
  between operations  0.64 us (2%)
    pallas_call x1, Pallas kernels, per_device(): pl.pallas_call(functools.partial(exchange, tiles, slots, fields, rows, co...  38.5 us
    pallas_call x1, Pallas kernels, per_device(): pl.pallas_call(functools.partial(finish, fields, rows, columns, sources),...  1.28 us

profile of v6, /device:TPU:1, one launch (start us, length us, event | category | flops | bytes accessed | tf_op | source)
XLA Modules:
  0.0 40.5 jit_solution(6377750471102195931)
XLA Ops:
  0.6 38.5 %shard_map.86 = (f32[512,16,128]{2,1,0:T(8,128)S(1)}, f32[2,512,128]{2,1,0:T(8,128)S(1)}, f32[32,256]{1,0:T(8,128)S(1)}, f32[1,16]{1,0:T(1,128)S(4)}, s32[4,64]{1,0:T(4,128)S(4)}) custom-call(f32[512,256]{1,0:T(8,128)} %bitcast.11, bf16[256,128,128]{2,1,0:T(8,128)(2,1)} %bitcast.10, s32[8,64]{1,0:T(8,128)} %bitcast.12, s32[4,64]{1,0:T(4,128)} %bitcast.13, ...), custom_call_target="tpu_custom_call" | custom-call | tf_op jit(solution)/shard_map/pallas_call | solution.py:246
  39.2 1.3 %shard_map.87 = (f32[16,32,256]{2,1,0:T(8,128)}, f32[16,32,256]{2,1,0:T(8,128)}) custom-call(f32[512,16,128]{2,1,0:T(8,128)S(1)} %get-tuple-element.9.products, f32[2,512,128]{2,1,0:T(8,128)S(1)} %get-tuple-element.10.stepped, f32[32,256]{1,0:T(8,128)S(1)} %get-tuple-element.11.cover, f32[1,16]{1,0:T(1,128)S(4)} %get-tuple-element.12.coupling_ref, ...), custom_call_target="tpu_custom_call" | custom-call | tf_op jit(solution)/shard_map/pallas_call | solution.py:279

commit v7 on v6

--- a/solution.py
+++ b/solution.py
@@ -13,12 +13,21 @@
 MESH = pl.DeviceIdType.MESH
 
 
+def target_tile_offset(step):
+    x, turn, part = step % 4, (step // 4 + 1) % 4, step // 16
+    y, z_hi, core = (x + turn) % 4, (x + turn + part) % 2, (part // 2 + x // 2) % 2
+    return z_hi * 32 + x * 8 + y * 2 + core
+
+
 def target_tile(me, step, tiles):
     if tiles != 64:
         return lax.rem(me + step, tiles)
-    x, turn, part = step % 4, step // 4 % 4, step // 16
-    y, z_hi, core = (x + turn) % 4, (x + turn + part) % 2, (part // 2 + x // 2) % 2
-    return me ^ (z_hi * 32 + x * 8 + y * 2 + core)
+    return me ^ target_tile_offset(step)
+
+
+def hops(tiles, step):
+    offset = target_tile_offset(step) if tiles == 64 else 0
+    return sum((0, 1, 2, 1)[offset // low % 4] for low in (2, 8))
 
 
 def exchange(
@@ -57,8 +66,7 @@
     for neighbour in (above, below):
         pl.semaphore_signal(barrier, inc=1, device_id=(comp, neighbour), device_id_type=MESH)
 
-    @pl.loop(0, tiles, unroll=tiles)
-    def _(step):
+    for step in sorted(range(tiles), key=functools.partial(hops, tiles), reverse=True):
         pl.semaphore_signal(
             barrier, inc=1, device_id=(other, target_tile(me, step, tiles)), device_id_type=MESH
         )

time: 40.8 us -> 40.7 us (level)
  no operation moved by 1% of the time
where the time goes in v7:
time: 40.7 us; the launch traced here: 40.2 us
  Pallas kernels  39.5 us (97%)
  between operations  0.64 us (2%)
    pallas_call x1, Pallas kernels, per_device(): pl.pallas_call(functools.partial(exchange, tiles, slots, fields, rows, co...  38.3 us
    pallas_call x1, Pallas kernels, per_device(): pl.pallas_call(functools.partial(finish, fields, rows, columns, sources),...  1.27 us

profile of v7, /device:TPU:1, one launch (start us, length us, event | category | flops | bytes accessed | tf_op | source)
XLA Modules:
  0.0 40.2 jit_solution(1937936487463828515)
XLA Ops:
  0.6 38.3 %shard_map.86 = (f32[512,16,128]{2,1,0:T(8,128)S(1)}, f32[2,512,128]{2,1,0:T(8,128)S(1)}, f32[32,256]{1,0:T(8,128)S(1)}, f32[1,16]{1,0:T(1,128)S(4)}, s32[4,64]{1,0:T(4,128)S(4)}) custom-call(f32[512,256]{1,0:T(8,128)} %bitcast.11, bf16[256,128,128]{2,1,0:T(8,128)(2,1)} %bitcast.10, s32[8,64]{1,0:T(8,128)} %bitcast.12, s32[4,64]{1,0:T(4,128)} %bitcast.13, ...), custom_call_target="tpu_custom_call" | custom-call | tf_op jit(solution)/shard_map/pallas_call | solution.py:254
  38.9 1.3 %shard_map.87 = (f32[16,32,256]{2,1,0:T(8,128)}, f32[16,32,256]{2,1,0:T(8,128)}) custom-call(f32[512,16,128]{2,1,0:T(8,128)S(1)} %get-tuple-element.9.products, f32[2,512,128]{2,1,0:T(8,128)S(1)} %get-tuple-element.10.stepped, f32[32,256]{1,0:T(8,128)S(1)} %get-tuple-element.11.cover, f32[1,16]{1,0:T(1,128)S(4)} %get-tuple-element.12.coupling_ref, ...), custom_call_target="tpu_custom_call" | custom-call | tf_op jit(solution)/shard_map/pallas_call | solution.py:287

commit v8 on v6

--- a/solution.py
+++ b/solution.py
@@ -211,14 +211,9 @@
             turned = jnp.swapaxes(jnp.stack(totals), 0, 1)
             for field in range(fields):
                 flux[half, pl.ds(field * rows + group * GROUP_ROWS, GROUP_ROWS)] = turned[field]
-        shares = cover[group * GROUP_ROWS:(group + 1) * GROUP_ROWS]
-        for field in range(fields):
-            lines = pl.ds(field * rows + group * GROUP_ROWS, GROUP_ROWS)
-            for half in range(halves):
-                share = coupling_ref[0, field] * shares[:, half * BLOCK:(half + 1) * BLOCK]
-                new[half, lines] = stepped[half, lines] + share * flux[half, lines]
         here = pl.ds(group * GROUP_ROWS, GROUP_ROWS)
-        for number, (source, target, sem) in enumerate(((new, new_hbm, new_sem), (flux, flux_hbm, flux_sem))):
+
+        def send(source, target, sem):
             for half in range(halves):
                 copy = pltpu.make_async_copy(
                     source.reshape(halves, fields, rows, BLOCK).at[half, :, here],
@@ -227,6 +222,15 @@
                 )
                 copy.start()
                 copies.append(copy)
+
+        send(flux, flux_hbm, flux_sem)
+        shares = cover[group * GROUP_ROWS:(group + 1) * GROUP_ROWS]
+        for field in range(fields):
+            lines = pl.ds(field * rows + group * GROUP_ROWS, GROUP_ROWS)
+            for half in range(halves):
+                share = coupling_ref[0, field] * shares[:, half * BLOCK:(half + 1) * BLOCK]
+                new[half, lines] = stepped[half, lines] + share * flux[half, lines]
+        send(new, new_hbm, new_sem)
     for copy in copies:
         copy.wait()
 

time: 40.8 us -> 40.8 us (level)
  no operation moved by 1% of the time
where the time goes in v8:
time: 40.8 us; the launch traced here: 40.5 us
  Pallas kernels  39.8 us (98%)
  between operations  0.64 us (2%)
    pallas_call x1, Pallas kernels, per_device(): pl.pallas_call(functools.partial(exchange, tiles, slots, fields, rows, co...  38.5 us
    pallas_call x1, Pallas kernels, per_device(): pl.pallas_call(functools.partial(finish, fields, rows, columns, sources),...  1.27 us

profile of v8, /device:TPU:1, one launch (start us, length us, event | category | flops | bytes accessed | tf_op | source)
XLA Modules:
  0.0 40.5 jit_solution(9359653441866721147)
XLA Ops:
  0.6 38.5 %shard_map.86 = (f32[512,16,128]{2,1,0:T(8,128)S(1)}, f32[2,512,128]{2,1,0:T(8,128)S(1)}, f32[32,256]{1,0:T(8,128)S(1)}, f32[1,16]{1,0:T(1,128)S(4)}, s32[4,64]{1,0:T(4,128)S(4)}) custom-call(f32[512,256]{1,0:T(8,128)} %bitcast.11, bf16[256,128,128]{2,1,0:T(8,128)(2,1)} %bitcast.10, s32[8,64]{1,0:T(8,128)} %bitcast.12, s32[4,64]{1,0:T(4,128)} %bitcast.13, ...), custom_call_target="tpu_custom_call" | custom-call | tf_op jit(solution)/shard_map/pallas_call | solution.py:250
  39.2 1.3 %shard_map.87 = (f32[16,32,256]{2,1,0:T(8,128)}, f32[16,32,256]{2,1,0:T(8,128)}) custom-call(f32[512,16,128]{2,1,0:T(8,128)S(1)} %get-tuple-element.9.products, f32[2,512,128]{2,1,0:T(8,128)S(1)} %get-tuple-element.10.stepped, f32[32,256]{1,0:T(8,128)S(1)} %get-tuple-element.11.cover, f32[1,16]{1,0:T(1,128)S(4)} %get-tuple-element.12.coupling_ref, ...), custom_call_target="tpu_custom_call" | custom-call | tf_op jit(solution)/shard_map/pallas_call | solution.py:283
